TPU v7x, 256 devices: a whole 4x4x8 slice. The times are simulated.
256 devices in a mesh: ctx: 32 (over y, x, z_lo), ch: 8 (over z_hi, core).
Axes of the slice: x: 4, y: 4, z: 8 (z_hi: 4, z_lo: 2; z = z_hi * 2 + z_lo), core: 2. Of those that a mesh axis runs over, the one named last changes fastest.
Arguments:
- tokens: bfloat16 [65536, 1024], P('ctx', 'ch'), may hold values from -6 to 6
- w_in: bfloat16 [1024, 1024], P(None, 'ch'), may hold values from -0.1875 to 0.1875
- filters: float32 [65536, 24], P('ctx'), may hold values from -0.0234375 to 0.0234375
- w_filter: float32 [24, 1024], P(None, 'ch'), may hold values from -1.25 to 1.25
- w_out: bfloat16 [1024, 1024], P('ch'), may hold values from -0.1875 to 0.1875
Outputs:
- output: bfloat16 [65536, 1024], P('ctx', 'ch')
All inputs are finite; a program needn't handle non-finite values.
Results may differ from a plain program's by a relative error of at most 0.0049.
Values may be sent and summed in bfloat16 or wider, within the bound.
No kernel may reach another device: no remote copies, remote signals or barrier semaphores. Data moves between devices by JAX's collectives and lax.ppermute only.
A program may use at most 64 MiB of HBM per device.

v0:
```python
import math
import jax
import jax.numpy as jnp
from jax import lax
from jax.sharding import PartitionSpec as P

COLS = 256
highest_mode = lax.Precision.HIGHEST


def cos_sin_table(left_index, right_index, period):
    phases = left_index[:, None] * right_index[None, :] % period
    angles = 2.0 * math.pi / period * phases.astype(jnp.float32)
    return (jnp.cos(angles), jnp.sin(angles))


def local(tokens, w_in, filters, w_filter, w_out):
    row_count, chan_count = tokens.shape
    ctx_count = lax.axis_size("ctx")
    ctx_place = lax.axis_index("ctx")
    inner_len = COLS
    outer_dev = row_count // inner_len
    outer_len = outer_dev * ctx_count
    padded_len = 2 * outer_len
    total_len = padded_len * inner_len
    inner_dev = inner_len // ctx_count
    projected = jnp.dot(
        lax.all_gather(tokens, "ch", axis=1, tiled=True), w_in, preferred_element_type=jnp.float32
    )
    shaped = jnp.dot(filters, w_filter, precision=highest_mode)
    signal = jnp.concatenate([projected, shaped], axis=1)
    signal = signal.reshape(outer_dev, inner_len, signal.shape[1])
    outer_index = jnp.arange(outer_len, dtype=jnp.int32)
    padded_index = jnp.arange(padded_len, dtype=jnp.int32)
    inner_index = jnp.arange(inner_len, dtype=jnp.int32)
    local_inner = ctx_place * inner_dev + jnp.arange(inner_dev, dtype=jnp.int32)
    outer_cos, outer_sin = cos_sin_table(padded_index, outer_index, padded_len)
    twiddle_cos, twiddle_sin = cos_sin_table(padded_index, local_inner, total_len)
    twiddle_cos = twiddle_cos[:, :, None]
    twiddle_sin = twiddle_sin[:, :, None]
    inner_cos, inner_sin = cos_sin_table(inner_index, inner_index, inner_len)
    block_part = lax.all_to_all(signal, "ctx", split_axis=1, concat_axis=0, tiled=True)
    real_part = jnp.einsum("kn,nbc->kbc", outer_cos, block_part, precision=highest_mode)
    imag_part = -jnp.einsum("kn,nbc->kbc", outer_sin, block_part, precision=highest_mode)
    first_spectra = jnp.stack(
        [
            real_part * twiddle_cos + imag_part * twiddle_sin,
            imag_part * twiddle_cos - real_part * twiddle_sin,
        ]
    )

    def inner_product(table, values):
        return jnp.einsum("kn,fnc->fkc", table, values, precision=highest_mode)

    block_part = lax.all_to_all(first_spectra, "ctx", split_axis=1, concat_axis=2, tiled=True)
    real_in = block_part[0]
    imag_in = block_part[1]
    real_out = inner_product(inner_cos, real_in) + inner_product(inner_sin, imag_in)
    imag_out = inner_product(inner_cos, imag_in) - inner_product(inner_sin, real_in)
    spectra = jnp.stack([real_out, imag_out])
    signal_re = spectra[0, :, :, :chan_count]
    signal_im = spectra[1, :, :, :chan_count]
    kernel = spectra[:, :, :, chan_count:]
    product_re = signal_re * kernel[0] - signal_im * kernel[1]
    product_im = signal_re * kernel[1] + signal_im * kernel[0]
    back_re = inner_product(inner_cos, product_re) - inner_product(inner_sin, product_im)
    back_im = inner_product(inner_cos, product_im) + inner_product(inner_sin, product_re)
    halfway = jnp.stack([back_re, back_im])
    block_part = lax.all_to_all(halfway, "ctx", split_axis=2, concat_axis=1, tiled=True)
    real_in = block_part[0]
    imag_in = block_part[1]
    turned_re = real_in * twiddle_cos - imag_in * twiddle_sin
    turned_im = imag_in * twiddle_cos + real_in * twiddle_sin
    summed = jnp.einsum("kn,kbc->nbc", outer_cos, turned_re, precision=highest_mode)
    summed = summed - jnp.einsum("kn,kbc->nbc", outer_sin, turned_im, precision=highest_mode)
    positions = summed * (1.0 / total_len)
    conv = (
        lax.all_to_all(
            positions.astype(jnp.bfloat16), "ctx", split_axis=0, concat_axis=1, tiled=True
        )
        .astype(positions.dtype)
        .reshape(row_count, chan_count)
    )
    mixed = conv.astype(jnp.bfloat16)
    partial_terms = jnp.dot(mixed, w_out, preferred_element_type=jnp.float32)
    result = lax.psum_scatter(partial_terms, "ch", scatter_dimension=1, tiled=True)
    return result.astype(jnp.bfloat16)


def solution(mesh):
    placed = (P("ctx", "ch"), P(None, "ch"), P("ctx", None), P(None, "ch"), P("ch", None))
    return jax.shard_map(
        local, mesh=mesh, in_specs=placed, out_specs=P("ctx", "ch"), check_vma=False
    )
```

profile of v0, /device:TPU:40, one launch (start us, length us, event | category | flops | bytes accessed | tf_op | source)
XLA Modules:
  0.0 496.1 jit_solution(14305966484975328182)
XLA Ops:
  6.5 0.0 all-gather.2.cloned.1.call-start
  6.5 0.7 all-gather.2.cloned.1.call-update
  7.3 1.9 fusion.152
  9.2 57.7 %all-gather.2.cloned.1.call-done = bf16[2048,1024]{1,0:T(8,128)(2,1)} async-done(((bf16[2048,128]{1,0:T(8,128)(2,1)}), bf16[2048,1024]{1,0:T(8,128)(2,1)}) %all-gather.2.cloned.1.call-update) | async-done | bytes 4194320 | tf_op jit(solution)/shard_map/all_gather | solution.py:28
  66.9 3.7 fusion.151
  70.6 0.1 pad_maximum_fusion.2
  70.8 0.9 copy.92
  71.7 2.1 copy.60
  73.7 9.4 %all-to-all-start = ((f32[8,256,256]{2,0,1:T(8,128)}), f32[8,256,256]{2,0,1:T(8,128)S(1)}, u32[]{:S(2)}, u32[]{:S(2)}) async-start(f32[8,256,256]{2,0,1:T(8,128)} %copy.60), calls=%async_computation | async-start | bytes 4194304 | tf_op jit(solution)/shard_map/all_to_all | solution.py:42
  83.2 0.2 fusion.96
  83.3 27.2 %all-to-all-done = f32[8,256,256]{2,0,1:T(8,128)S(1)} async-done(((f32[8,256,256]{2,0,1:T(8,128)}), f32[8,256,256]{2,0,1:T(8,128)S(1)}, u32[]{:S(2)}, u32[]{:S(2)}) %all-to-all-start) | async-done | bytes 2097184 | tf_op jit(solution)/shard_map/all_to_all | solution.py:42
  110.5 5.8 %fusion.26 = f32[512,8,256]{2,0,1:T(8,128)S(1)} fusion(f32[32,8,8,256]{3,1,2,0:T(8,128)S(1)} %bitcast.127), kind=kOutput, calls=%fused_computation.34 | convolution fusion | flops 3223060480 | bytes 6291456 | tf_op jit(solution)/shard_map/kn,nbc->kbc/dot_general | solution.py:44
  116.3 20.1 %add_bitcast_fusion.1 = (f32[1,512,8,256]{3,1,2,0:T(8,128)S(1)}, f32[1,512,8,256]{3,1,2,0:T(8,128)S(1)}) fusion(f32[512,8,256]{2,0,1:T(8,128)S(1)} %fusion.26, f32[512,8]{0,1:T(8,128)S(1)} %get-tuple-element.16, f32[512,8]{0,1:T(8,128)S(1)} %get-tuple-element.15, f32[32,8,8,256]{3,1,2,0:T(8,128)S(1)} %bitcast.128), kind=kOutput, calls=%fused_computation.14 | convolution fusion | flops 3230400512 | bytes 14712832 | tf_op jit(solution)/shard_map/kn,nbc->kbc/dot_general | solution.py:43
  136.4 0.7 pad_maximum_fusion
  137.1 4.9 copy.65
  142.0 100.5 %all_to_all.66 = f32[2,512,8,256]{3,2,0,1:T(8,128)S(1)} all-to-all(f32[2,512,8,256]{3,2,0,1:T(8,128)S(1)} %copy.65), channel_id=1, replica_groups=mesh['ctx'=32,'ch'=8] {'ctx'}, dimensions={1} | all-to-all | bytes 16777216 | tf_op jit(solution)/shard_map/all_to_all | solution.py:55
  242.5 0.7 copy.66
  243.2 1.0 fusion.145
  244.2 7.9 %fusion.2 = f32[16,256,256]{2,1,0:T(8,128)S(1)} fusion(f32[1,16,32,8,256]{4,3,1,2,0:T(8,128)S(1)} %get-tuple-element.10), kind=kOutput, calls=%fused_computation.4 | convolution fusion | flops 3222142976 | bytes 8388608 | tf_op jit(solution)/shard_map/kn,fnc->fkc/dot_general | solution.py:53
  252.1 8.4 %fusion = f32[16,256,256]{2,1,0:T(8,128)S(1)} fusion(f32[1,16,32,8,256]{4,3,1,2,0:T(8,128)S(1)} %get-tuple-element.10), kind=kOutput, calls=%fused_computation.2 | convolution fusion | flops 3222142976 | bytes 8388608 | tf_op jit(solution)/shard_map/kn,fnc->fkc/dot_general | solution.py:53
  260.5 8.3 %add_bitcast_fusion = f32[1,16,256,256]{2,3,1,0:T(8,128)S(1)} fusion(f32[16,256,256]{2,1,0:T(8,128)S(1)} %fusion.2, f32[1,16,32,8,256]{4,3,1,2,0:T(8,128)S(1)} %get-tuple-element.9), kind=kOutput, calls=%fused_computation.12 | convolution fusion | flops 3223191552 | bytes 12582912 | tf_op jit(solution)/shard_map/kn,fnc->fkc/dot_general | solution.py:53
  268.8 8.3 %subtract_bitcast_fusion = f32[1,16,256,256]{2,3,1,0:T(8,128)S(1)} fusion(f32[16,256,256]{2,1,0:T(8,128)S(1)} %fusion, f32[1,16,32,8,256]{4,3,1,2,0:T(8,128)S(1)} %get-tuple-element.9), kind=kOutput, calls=%fused_computation.11 | convolution fusion | flops 3223191552 | bytes 12582912 | tf_op jit(solution)/shard_map/kn,fnc->fkc/dot_general | solution.py:53
  277.1 0.7 multiply_subtract_fusion
  277.8 2.8 fusion.20
  280.6 3.0 fusion.18
  283.7 2.9 subtract_bitcast_fusion.2
  286.6 2.9 add_bitcast_fusion.2
  289.4 2.3 pad_maximum_fusion.1
  291.8 5.5 %copy.73 = f32[2,16,256,128]{3,1,0,2:T(8,128)} copy(f32[2,16,256,128]{2,3,1,0:T(8,128)} %pad_maximum_fusion.1) | data formatting | bytes 8388608 | tf_op jit(solution)/shard_map/stack | solution.py:68
  297.2 7.2 %all-to-all-start.2 = ((f32[2,16,256,128]{3,1,0,2:T(8,128)}), f32[2,16,256,128]{3,1,0,2:T(8,128)}, u32[]{:S(2)}, u32[]{:S(2)}) async-start(f32[2,16,256,128]{3,1,0,2:T(8,128)} %copy.73), calls=%async_computation.2 | async-start | bytes 8388608 | tf_op jit(solution)/shard_map/all_to_all | solution.py:69
  304.4 0.3 reduce-scatter.2.cloned.1.call-start
  304.7 0.1 copy.76
  304.8 0.1 copy.78
  305.0 49.1 %all-to-all-done.2 = f32[2,16,256,128]{3,1,0,2:T(8,128)} async-done(((f32[2,16,256,128]{3,1,0,2:T(8,128)}), f32[2,16,256,128]{3,1,0,2:T(8,128)}, u32[]{:S(2)}, u32[]{:S(2)}) %all-to-all-start.2) | async-done | bytes 4194336 | tf_op jit(solution)/shard_map/all_to_all | solution.py:69
  354.1 4.6 copy.134
  358.7 0.4 fusion.146
  359.2 0.3 copy.75
  359.4 0.3 copy.77
  359.7 1.6 fusion.16
  361.3 3.9 fusion.30
  365.3 4.0 fusion.46
  369.3 0.3 copy.81
  369.6 15.6 %all_to_all.67 = bf16[256,8,128]{2,1,0:T(8,128)(2,1)S(1)} all-to-all(bf16[256,8,128]{2,1,0:T(8,128)(2,1)S(1)} %copy.81), channel_id=1, replica_groups=mesh['ctx'=32,'ch'=8] {'ctx'}, dimensions={0} | all-to-all | bytes 1048576 | tf_op jit(solution)/shard_map/all_to_all | solution.py:78
  385.3 0.1 copy.82
  385.4 4.5 fusion.153
  389.8 0.0 reduce-scatter.2.cloned.1.call-update
  389.9 96.9 %reduce-scatter.2.cloned.1.call-done = f32[2048,128]{1,0:T(8,128)} async-done(((f32[2048,1024]{1,0:T(8,128)}), f32[2048,128]{1,0:T(8,128)}) %reduce-scatter.2.cloned.1.call-update) | async-done | bytes 1048592 | tf_op jit(solution)/shard_map/reduce_scatter | solution.py:86
  486.8 2.1 convert_element_type.49
  (3 shorter events, 0.0 us)
Async XLA Ops:
  6.5 378.8 %copy-start = (bf16[128,1024]{1,0:T(8,128)(2,1)S(1)}, bf16[128,1024]{1,0:T(8,128)(2,1)}, u32[]{:S(2)}) copy-start(bf16[128,1024]{1,0:T(8,128)(2,1)} %param.9) | copy-start | bytes 786436
  6.5 60.4 %all-gather.2.cloned.1.call-start = ((), (), s32[]{:S(2)}) async-start(), calls=%async_computation.5 | async-start | bytes 4718592 | tf_op jit(solution)/shard_map/all_gather | solution.py:28
  73.7 36.8 %all-to-all-start = ((f32[8,256,256]{2,0,1:T(8,128)}), f32[8,256,256]{2,0,1:T(8,128)S(1)}, u32[]{:S(2)}, u32[]{:S(2)}) async-start(f32[8,256,256]{2,0,1:T(8,128)} %copy.60), calls=%async_computation | async-start | bytes 4194304 | tf_op jit(solution)/shard_map/all_to_all | solution.py:42
  297.2 56.9 %all-to-all-start.2 = ((f32[2,16,256,128]{3,1,0,2:T(8,128)}), f32[2,16,256,128]{3,1,0,2:T(8,128)}, u32[]{:S(2)}, u32[]{:S(2)}) async-start(f32[2,16,256,128]{3,1,0,2:T(8,128)} %copy.73), calls=%async_computation.2 | async-start | bytes 8388608 | tf_op jit(solution)/shard_map/all_to_all | solution.py:69
  304.4 182.4 %reduce-scatter.2.cloned.1.call-start = ((), (), s32[]{:S(2)}) async-start(), calls=%async_computation.6 | async-start | bytes 9437184 | tf_op jit(solution)/shard_map/reduce_scatter | solution.py:86
Sparse Core Ops, SparseCore 0:
  9.2 57.6 all-gather.1
  390.0 96.7 reduce-scatter.1
where the time goes:
time: 500 us; the launch traced here: 496 us
  waiting for transfers between devices  232 us (46%)
  blocking collectives  116 us (23%)
  matrix products  88.4 us (18%)
  local copies, waits for them, and re-layouts  21.2 us (4%)
  starting transfers between devices  16.9 us (3%)
  between operations  14.1 us (3%)
  other arithmetic  7.71 us (2%)
    all_to_all x1, blocking collectives, local(): lax.all_to_all(first_spectra, 'ctx', split_axis=1, concat_axis=2, tiled=T...  101 us
    reduce_scatter x1, waiting for transfers between devices, local(): lax.psum_scatter(partial_terms, 'ch', scatter_dimension=1, tiled=True)  96.9 us
    all_gather x1, waiting for transfers between devices, local(): lax.all_gather(tokens, 'ch', axis=1, tiled=True)  57.7 us
    all_to_all x1, waiting for transfers between devices, local(): lax.all_to_all(halfway, 'ctx', split_axis=2, concat_axis=1, tiled=True)  49.1 us
    dot_general x8, matrix products, inner_product(): return jnp.einsum('kn,fnc->fkc', table, values, precision=highest_mode)  44.5 us
    all_to_all x1, waiting for transfers between devices, local(): lax.all_to_all(signal, 'ctx', split_axis=1, concat_axis=0, tiled=True)  27.2 us
    dot_general x1, matrix products, local(): jnp.einsum('kn,nbc->kbc', outer_cos, block_part, precision=highest_mode)  20.1 us
    all_to_all x1, blocking collectives, local(): lax.all_to_all(positions.astype(jnp.bfloat16), 'ctx', split_axis=0, conca...  15.6 us
  transfers between devices with their start and end apart: 4, of which 4 were waited for; matrix products, arithmetic and copies ran while one was open for 0% of the time, Pallas kernels for 0%

commit v1 on v0

--- a/solution.py
+++ b/solution.py
@@ -25,7 +25,11 @@
     total_len = padded_len * inner_len
     inner_dev = inner_len // ctx_count
     projected = jnp.dot(
-        lax.all_gather(tokens, "ch", axis=1, tiled=True), w_in, preferred_element_type=jnp.float32
+        jnp.concatenate(
+            lax.all_to_all(jnp.stack([tokens] * lax.axis_size("ch")), "ch", 0, 0), axis=1
+        ),
+        w_in,
+        preferred_element_type=jnp.float32,
     )
     shaped = jnp.dot(filters, w_filter, precision=highest_mode)
     signal = jnp.concatenate([projected, shaped], axis=1)

time: 500 us -> 542 us (1.084)
  waiting for transfers between devices: 232 us -> 266 us
  starting transfers between devices: 16.9 us -> 24 us
    all_to_all x0 -> x1, waiting for transfers between devices: none -> 95.7 us  [local(): lax.all_to_all(jnp.stack([tokens] * lax.axis_size('ch')), 'ch', 0, 0)]
    all_gather x1 -> x0, waiting for transfers between devices: 57.7 us -> none  [local(): lax.all_gather(tokens, 'ch', axis=1, tiled=True)]
    all_to_all x0 -> x1, starting transfers between devices: none -> 7.7 us  [local(): lax.all_to_all(jnp.stack([tokens] * lax.axis_size('ch')), 'ch', 0, 0)]
where the time goes in v1:
time: 542 us; the launch traced here: 538 us
  waiting for transfers between devices  266 us (49%)
  blocking collectives  114 us (21%)
  matrix products  86.7 us (16%)
  local copies, waits for them, and re-layouts  25 us (5%)
  starting transfers between devices  24 us (4%)
  between operations  14.1 us (3%)
  other arithmetic  7.75 us (1%)
    all_to_all x1, blocking collectives, local(): lax.all_to_all(first_spectra, 'ctx', split_axis=1, concat_axis=2, tiled=T...  98.2 us
    all_to_all x1, waiting for transfers between devices, local(): lax.all_to_all(jnp.stack([tokens] * lax.axis_size('ch')), 'ch', 0, 0)  95.7 us
    reduce_scatter x1, waiting for transfers between devices, local(): lax.psum_scatter(partial_terms, 'ch', scatter_dimension=1, tiled=True)  94.5 us
    all_to_all x1, waiting for transfers between devices, local(): lax.all_to_all(halfway, 'ctx', split_axis=2, concat_axis=1, tiled=True)  48.8 us
    dot_general x8, matrix products, inner_product(): return jnp.einsum('kn,fnc->fkc', table, values, precision=highest_mode)  44.5 us
    all_to_all x1, waiting for transfers between devices, local(): lax.all_to_all(signal, 'ctx', split_axis=1, concat_axis=0, tiled=True)  26.9 us
    dot_general x1, matrix products, local(): jnp.einsum('kn,nbc->kbc', outer_cos, block_part, precision=highest_mode)  20.1 us
    all_to_all x1, blocking collectives, local(): lax.all_to_all(positions.astype(jnp.bfloat16), 'ctx', split_axis=0, conca...  16 us
  transfers between devices with their start and end apart: 4, of which 4 were waited for; matrix products, arithmetic and copies ran while one was open for 0% of the time, Pallas kernels for 0%

profile of v1, /device:TPU:40, one launch (start us, length us, event | category | flops | bytes accessed | tf_op | source)
XLA Modules:
  0.0 537.7 jit_solution(5009540644270513253)
XLA Ops:
  6.5 1.3 copy.63
  7.8 2.5 stack.36
  10.4 7.7 %all-to-all-start = ((bf16[8,2048,128]{1,2,0:T(8,128)(2,1)}), bf16[8,2048,128]{1,2,0:T(8,128)(2,1)}, u32[]{:S(2)}, u32[]{:S(2)}) async-start(bf16[8,2048,128]{1,2,0:T(8,128)(2,1)} %stack.36), calls=%async_computation | async-start | bytes 8388608 | tf_op jit(solution)/shard_map/all_to_all | solution.py:29
  18.1 1.0 fusion.152
  19.1 95.7 %all-to-all-done = bf16[8,2048,128]{1,2,0:T(8,128)(2,1)} async-done(((bf16[8,2048,128]{1,2,0:T(8,128)(2,1)}), bf16[8,2048,128]{1,2,0:T(8,128)(2,1)}, u32[]{:S(2)}, u32[]{:S(2)}) %all-to-all-start) | async-done | bytes 4194336 | tf_op jit(solution)/shard_map/all_to_all | solution.py:29
  114.8 2.9 fusion.151
  117.8 0.2 pad_maximum_fusion.2
  118.0 0.9 copy.96
  118.9 2.1 copy.64
  120.9 8.8 %all-to-all-start.1 = ((f32[8,256,256]{2,0,1:T(8,128)}), f32[8,256,256]{2,0,1:T(8,128)S(1)}, u32[]{:S(2)}, u32[]{:S(2)}) async-start(f32[8,256,256]{2,0,1:T(8,128)} %copy.64), calls=%async_computation.1 | async-start | bytes 4194304 | tf_op jit(solution)/shard_map/all_to_all | solution.py:46
  129.8 0.2 fusion.96
  129.9 26.9 %all-to-all-done.1 = f32[8,256,256]{2,0,1:T(8,128)S(1)} async-done(((f32[8,256,256]{2,0,1:T(8,128)}), f32[8,256,256]{2,0,1:T(8,128)S(1)}, u32[]{:S(2)}, u32[]{:S(2)}) %all-to-all-start.1) | async-done | bytes 2097184 | tf_op jit(solution)/shard_map/all_to_all | solution.py:46
  156.8 5.8 %fusion.26 = f32[512,8,256]{2,0,1:T(8,128)S(1)} fusion(f32[32,8,8,256]{3,1,2,0:T(8,128)S(1)} %bitcast.130), kind=kOutput, calls=%fused_computation.34 | convolution fusion | flops 3223060480 | bytes 6291456 | tf_op jit(solution)/shard_map/kn,nbc->kbc/dot_general | solution.py:48
  162.6 20.1 %add_bitcast_fusion.1 = (f32[1,512,8,256]{3,1,2,0:T(8,128)S(1)}, f32[1,512,8,256]{3,1,2,0:T(8,128)S(1)}) fusion(f32[512,8,256]{2,0,1:T(8,128)S(1)} %fusion.26, f32[512,8]{0,1:T(8,128)S(1)} %get-tuple-element.16, f32[512,8]{0,1:T(8,128)S(1)} %get-tuple-element.15, f32[32,8,8,256]{3,1,2,0:T(8,128)S(1)} %bitcast.131), kind=kOutput, calls=%fused_computation.14 | convolution fusion | flops 3230400512 | bytes 14712832 | tf_op jit(solution)/shard_map/kn,nbc->kbc/dot_general | solution.py:47
  182.7 0.7 pad_maximum_fusion
  183.5 4.9 copy.69
  188.3 98.2 %all_to_all.71 = f32[2,512,8,256]{3,2,0,1:T(8,128)S(1)} all-to-all(f32[2,512,8,256]{3,2,0,1:T(8,128)S(1)} %copy.69), channel_id=1, replica_groups=mesh['ctx'=32,'ch'=8] {'ctx'}, dimensions={1} | all-to-all | bytes 16777216 | tf_op jit(solution)/shard_map/all_to_all | solution.py:59
  286.5 0.7 copy.70
  287.2 1.0 fusion.145
  288.1 7.9 %fusion.2 = f32[16,256,256]{2,1,0:T(8,128)S(1)} fusion(f32[1,16,32,8,256]{4,3,1,2,0:T(8,128)S(1)} %get-tuple-element.10), kind=kOutput, calls=%fused_computation.4 | convolution fusion | flops 3222142976 | bytes 8388608 | tf_op jit(solution)/shard_map/kn,fnc->fkc/dot_general | solution.py:57
  296.1 8.4 %fusion = f32[16,256,256]{2,1,0:T(8,128)S(1)} fusion(f32[1,16,32,8,256]{4,3,1,2,0:T(8,128)S(1)} %get-tuple-element.10), kind=kOutput, calls=%fused_computation.2 | convolution fusion | flops 3222142976 | bytes 8388608 | tf_op jit(solution)/shard_map/kn,fnc->fkc/dot_general | solution.py:57
  304.5 8.3 %add_bitcast_fusion = f32[1,16,256,256]{2,3,1,0:T(8,128)S(1)} fusion(f32[16,256,256]{2,1,0:T(8,128)S(1)} %fusion.2, f32[1,16,32,8,256]{4,3,1,2,0:T(8,128)S(1)} %get-tuple-element.9), kind=kOutput, calls=%fused_computation.12 | convolution fusion | flops 3223191552 | bytes 12582912 | tf_op jit(solution)/shard_map/kn,fnc->fkc/dot_general | solution.py:57
  312.8 8.3 %subtract_bitcast_fusion = f32[1,16,256,256]{2,3,1,0:T(8,128)S(1)} fusion(f32[16,256,256]{2,1,0:T(8,128)S(1)} %fusion, f32[1,16,32,8,256]{4,3,1,2,0:T(8,128)S(1)} %get-tuple-element.9), kind=kOutput, calls=%fused_computation.11 | convolution fusion | flops 3223191552 | bytes 12582912 | tf_op jit(solution)/shard_map/kn,fnc->fkc/dot_general | solution.py:57
  321.1 0.7 multiply_subtract_fusion
  321.8 2.8 fusion.20
  324.6 3.0 fusion.18
  327.7 2.9 subtract_bitcast_fusion.2
  330.5 2.9 add_bitcast_fusion.2
  333.4 2.3 pad_maximum_fusion.1
  335.7 5.5 %copy.77 = f32[2,16,256,128]{3,1,0,2:T(8,128)} copy(f32[2,16,256,128]{2,3,1,0:T(8,128)} %pad_maximum_fusion.1) | data formatting | bytes 8388608 | tf_op jit(solution)/shard_map/stack | solution.py:72
  341.2 7.2 %all-to-all-start.3 = ((f32[2,16,256,128]{3,1,0,2:T(8,128)}), f32[2,16,256,128]{3,1,0,2:T(8,128)}, u32[]{:S(2)}, u32[]{:S(2)}) async-start(f32[2,16,256,128]{3,1,0,2:T(8,128)} %copy.77), calls=%async_computation.3 | async-start | bytes 8388608 | tf_op jit(solution)/shard_map/all_to_all | solution.py:73
  348.4 0.3 reduce-scatter.2.cloned.1.call-start
  348.7 0.1 copy.80
  348.8 0.1 copy.82
  349.0 48.8 %all-to-all-done.3 = f32[2,16,256,128]{3,1,0,2:T(8,128)} async-done(((f32[2,16,256,128]{3,1,0,2:T(8,128)}), f32[2,16,256,128]{3,1,0,2:T(8,128)}, u32[]{:S(2)}, u32[]{:S(2)}) %all-to-all-start.3) | async-done | bytes 4194336 | tf_op jit(solution)/shard_map/all_to_all | solution.py:73
  397.8 4.6 copy.138
  402.4 0.4 fusion.146
  402.8 0.3 copy.79
  403.1 0.3 copy.81
  403.3 1.6 fusion.16
  405.0 3.9 fusion.30
  408.9 4.0 fusion.46
  412.9 0.3 copy.85
  413.3 16.0 %all_to_all.72 = bf16[256,8,128]{2,1,0:T(8,128)(2,1)S(1)} all-to-all(bf16[256,8,128]{2,1,0:T(8,128)(2,1)S(1)} %copy.85), channel_id=1, replica_groups=mesh['ctx'=32,'ch'=8] {'ctx'}, dimensions={0} | all-to-all | bytes 1048576 | tf_op jit(solution)/shard_map/all_to_all | solution.py:82
  429.2 0.1 copy.86
  429.3 4.5 fusion.153
  433.8 94.5 %reduce-scatter.2.cloned.1.call-done = f32[2048,128]{1,0:T(8,128)} async-done(((f32[2048,1024]{1,0:T(8,128)}), f32[2048,128]{1,0:T(8,128)}) %reduce-scatter.2.cloned.1.call-update) | async-done | bytes 1048592 | tf_op jit(solution)/shard_map/reduce_scatter | solution.py:90
  528.3 2.1 convert_element_type.49
  (10 shorter events, 0.0 us)
Async XLA Ops:
  6.5 422.8 %copy-start = (bf16[128,1024]{1,0:T(8,128)(2,1)S(1)}, bf16[128,1024]{1,0:T(8,128)(2,1)}, u32[]{:S(2)}) copy-start(bf16[128,1024]{1,0:T(8,128)(2,1)} %param.9) | copy-start | bytes 786436
  10.4 7.7 %copy-start.2 = (f32[2048,24]{0,1:T(8,128)S(1)}, f32[2048,24]{0,1:T(8,128)}, u32[]{:S(2)}) copy-start(f32[2048,24]{0,1:T(8,128)} %param.7) | copy-start | bytes 589828
  10.4 7.7 %copy-start.3 = (f32[24,128]{1,0:T(8,128)S(1)}, f32[24,128]{1,0:T(8,128)}, u32[]{:S(2)}) copy-start(f32[24,128]{1,0:T(8,128)} %param.8) | copy-start | bytes 36868
  10.4 104.5 %copy-start.1 = (bf16[1024,128]{1,0:T(8,128)(2,1)S(1)}, bf16[1024,128]{1,0:T(8,128)(2,1)}, u32[]{:S(2)}) copy-start(bf16[1024,128]{1,0:T(8,128)(2,1)} %param.6) | copy-start | bytes 786436
  10.4 104.5 %all-to-all-start = ((bf16[8,2048,128]{1,2,0:T(8,128)(2,1)}), bf16[8,2048,128]{1,2,0:T(8,128)(2,1)}, u32[]{:S(2)}, u32[]{:S(2)}) async-start(bf16[8,2048,128]{1,2,0:T(8,128)(2,1)} %stack.36), calls=%async_computation | async-start | bytes 8388608 | tf_op jit(solution)/shard_map/all_to_all | solution.py:29
  120.9 35.9 %all-to-all-start.1 = ((f32[8,256,256]{2,0,1:T(8,128)}), f32[8,256,256]{2,0,1:T(8,128)S(1)}, u32[]{:S(2)}, u32[]{:S(2)}) async-start(f32[8,256,256]{2,0,1:T(8,128)} %copy.64), calls=%async_computation.1 | async-start | bytes 4194304 | tf_op jit(solution)/shard_map/all_to_all | solution.py:46
  341.2 56.5 %all-to-all-start.3 = ((f32[2,16,256,128]{3,1,0,2:T(8,128)}), f32[2,16,256,128]{3,1,0,2:T(8,128)}, u32[]{:S(2)}, u32[]{:S(2)}) async-start(f32[2,16,256,128]{3,1,0,2:T(8,128)} %copy.77), calls=%async_computation.3 | async-start | bytes 8388608 | tf_op jit(solution)/shard_map/all_to_all | solution.py:73
  348.4 179.9 %reduce-scatter.2.cloned.1.call-start = ((), (), s32[]{:S(2)}) async-start(), calls=%async_computation.6 | async-start | bytes 9437184 | tf_op jit(solution)/shard_map/reduce_scatter | solution.py:90
Sparse Core Ops, SparseCore 0:
  434.0 94.2 reduce-scatter.1
